TPU v7x, 128 devices: a whole 4x4x4 slice. The times are simulated.
128 devices in a mesh: slab: 32 (over z, x, core), col: 4 (over y).
Axes of the slice: x: 4, y: 4, z: 4, core: 2. Of those that a mesh axis runs over, the one named last changes fastest.
Arguments:
- charge: float32 [512, 256, 512], P('slab', 'col'), may hold values from -0.6 to 0.6
Outputs:
- potential: float32 [512, 256, 512], P('slab', 'col')
All inputs are finite; a program needn't handle non-finite values.
Results may differ from a plain program's by a relative error of at most 0.000068.
Values sent between devices are 32-bit elements; how exact they have to be, the bound alone decides.
A program may use at most 128 MiB of HBM per device.

v0:
```python
import functools

import jax
import jax.numpy as jnp
from jax import lax
from jax.experimental import pallas as pl
from jax.experimental.pallas import tpu as pltpu
from jax.sharding import PartitionSpec as P

COARSE_SWEEPS = 12
KAPPA = 0.001
OMEGA = 0.8
FOUR_PI = 12.566370614359172
MESH = pl.DeviceIdType.MESH
F32 = jnp.float32


class Level:
    def __init__(self, scale):
        self.c = OMEGA / (6.0 * scale + KAPPA)
        self.a = 1.0 - OMEGA
        self.b = self.c * scale
        self.r = self.a / self.b
        self.t = 2.0 * self.b * self.b
        self.rho = self.r + 2.0
        self.alpha = (self.a**2 + 6.0 * self.a * self.b + 12.0 * self.b**2) / self.t


L0, L1, L2 = Level(1.0), Level(0.25), Level(0.0625)
SIGMA1 = FOUR_PI * L0.t / 8.0
SIGMA2 = SIGMA1 * L1.t / 8.0


def lane_of(n):
    return lax.broadcasted_iota(jnp.int32, (n, 128), 1)


def take(v, idx):
    return jnp.take_along_axis(v, idx, axis=1, mode="promise_in_bounds")


def shift_tables(n):
    lane = lane_of(n)
    up = jnp.where(lane < 124, lane + 4, (lane + 1) % 4)
    down = jnp.where(lane < 4, 124 + (lane + 3) % 4, lane - 4)
    return up, down


def x_up(v, up):
    return v[1:] + [take(v[0], up)]


def x_down(v, down):
    return [take(v[-1], down)] + v[:-1]


def swap(p, q, bit, lane):
    clear = (lane & bit) == 0
    t = take(jnp.where(clear, q, p), lane ^ bit)
    return jnp.where(clear, p, t), jnp.where(clear, t, q)


def to_groups(v, lane):
    a0, a1 = swap(v[0], v[1], 1, lane)
    a2, a3 = swap(v[2], v[3], 1, lane)
    b0, b2 = swap(a0, a2, 2, lane)
    b1, b3 = swap(a1, a3, 2, lane)
    return [b0, b1, b2, b3]


def from_groups(v, lane):
    b0, b2 = swap(v[0], v[2], 2, lane)
    b1, b3 = swap(v[1], v[3], 2, lane)
    a0, a1 = swap(b0, b1, 1, lane)
    a2, a3 = swap(b2, b3, 1, lane)
    return [a0, a1, a2, a3]


def add(*lists):
    out = lists[0]
    for l in lists[1:]:
        out = [a + b for a, b in zip(out, l)]
    return out


def mul(k, v):
    return [k * a for a in v]


def restrict_parts(load, lv, up, down):
    E, V = {}, {}
    for pz in (0, 1):
        for py in (0, 1):
            lo, hi = load(pz, py)
            E[pz, py] = add(lo, hi)
            V[pz, py] = add(x_up(lo, up), x_down(hi, down))
    K = {k: add(mul(lv.rho, E[k]), V[k]) for k in E}
    p = add(E[0, 0], E[0, 1], E[1, 0], E[1, 1])
    hp = mul(0.5, p)
    n0 = add(mul(lv.alpha, p), x_up(hp, up), x_down(hp, down))
    n0 = add(n0, mul(lv.rho, add(V[0, 0], V[0, 1], V[1, 0], V[1, 1])))
    nu = add(hp, K[0, 0], K[1, 0])
    nd = add(hp, K[0, 1], K[1, 1])
    zu = add(hp, K[0, 0], K[0, 1])
    zd = add(hp, K[1, 0], K[1, 1])
    return [n0, nu, nd, zu, E[0, 0], E[0, 1], zd, E[1, 0], E[1, 1]]


def gather_parts(T, z, j, row, n):
    here, above, below = pl.ds(row, n), pl.ds(row + 1, n), pl.ds(row - 1, n)
    out = T[0, z, j, here, :] + T[3, z + 1, j, here, :] + T[6, z - 1, j, here, :]
    out = out + (T[1, z, j, above, :] + T[4, z + 1, j, above, :] + T[7, z - 1, j, above, :])
    return out + (T[2, z, j, below, :] + T[5, z + 1, j, below, :] + T[8, z - 1, j, below, :])


def prolong_parts(q, lv, up, down):
    c = q(0, 0)
    zs, ys = (q(-1, 0), q(1, 0)), (q(0, -1), q(0, 1))
    n = add(zs[0], zs[1], ys[0], ys[1], x_up(c, up), x_down(c, down))
    n = add(mul(lv.alpha, c), mul(0.5, n))
    rc = mul(lv.rho, c)
    out = {}
    for pz in (0, 1):
        for py in (0, 1):
            s = add(zs[pz], ys[py])
            w = add(rc, s)
            A = add(n, mul(lv.rho, s), q(2 * pz - 1, 2 * py - 1))
            lo, hi = add(A, x_down(w, down)), add(A, x_up(w, up))
            out[pz, py] = [v for pair in zip(lo, hi) for v in pair]
    return out


def source_kernel(x_ref, f_ref, s1_ref, s2_ref, T0, T1):
    step = pl.program_id(0)
    planes = x_ref.shape[0]
    lane = lane_of(8)
    up, down = shift_tables(8)

    @pl.when(step == 0)
    def _():
        def clear(i, _):
            for z in (0, 1, 10, 11):
                T0[i, z] = jnp.zeros((2, 64, 128), F32)
            for z in range(2, 10):
                T0[i, z, :, 0:16, :] = jnp.zeros((2, 16, 128), F32)
                T0[i, z, :, 48:64, :] = jnp.zeros((2, 16, 128), F32)
            T1[i] = jnp.zeros(T1.shape[1:], F32)
            return 0

        lax.fori_loop(0, 9, clear, 0)
        s1_ref[0] = jnp.zeros(s1_ref.shape[1:], F32)
        s1_ref[11] = jnp.zeros(s1_ref.shape[1:], F32)

    def reorder(z, _):
        for r in range(0, 64, 8):
            v = [x_ref[z, pl.ds(r, 8), pl.ds(128 * k, 128)] for k in range(4)]
            for j, w in enumerate(to_groups(v, lane)):
                f_ref[z, j, pl.ds(r, 8), :] = w
        return 0

    lax.fori_loop(0, planes, reorder, 0, unroll=2)

    def parts0(i, _):
        for y in range(0, 32, 8):

            def load(pz, py):
                rows = pl.ds(2 * y + py, 8, stride=2)
                v = [f_ref[2 * i + pz, j, rows, :] for j in range(4)]
                return v[0::2], v[1::2]

            for k, part in enumerate(restrict_parts(load, L0, up, down)):
                for j, v in enumerate(part):
                    T0[k, step * (planes // 2) + i + 2, j, pl.ds(16 + y, 8), :] = v
        return 0

    lax.fori_loop(0, planes // 2, parts0, 0, unroll=True)

    @pl.when(step == pl.num_programs(0) - 1)
    def _():
        def sums0(z, _):
            for j in (0, 1):
                for r in range(0, 48, 8):
                    s1_ref[z, j, pl.ds(r, 8), :] = gather_parts(T0, z, j, r + 8, 8)
            return 0

        lax.fori_loop(1, 11, sums0, 0, unroll=2)

        def parts1(i, _):
            for y in (-4, 4, 12):

                def load(pz, py):
                    rows = pl.ds(2 * y + py + 8, 8, stride=2)
                    v = [s1_ref[2 * i + pz, j, rows, :] for j in (0, 1)]
                    return v[0:1], v[1:2]

                for k, part in enumerate(restrict_parts(load, L1, up, down)):
                    T1[k, i + 2, 0, pl.ds(16 + y, 8), :] = part[0]
            return 0

        lax.fori_loop(0, 6, parts1, 0, unroll=True)

        def sums1(z, _):
            for r in range(0, 32, 8):
                s2_ref[z, pl.ds(r, 8), :] = gather_parts(T1, z + 1, 0, r + 8, 8)
            return 0

        lax.fori_loop(0, 8, sums1, 0, unroll=2)


def local_sources(charge):
    step = 4
    return pl.pallas_call(
        source_kernel,
        grid=(16 // step,),
        in_specs=[pl.BlockSpec((step, 64, 512), lambda i: (i, 0, 0))],
        out_specs=[
            pl.BlockSpec((step, 4, 64, 128), lambda i: (i, 0, 0, 0)),
            pl.BlockSpec((12, 2, 48, 128), lambda i: (0, 0, 0, 0)),
            pl.BlockSpec((8, 32, 128), lambda i: (0, 0, 0)),
        ],
        out_shape=[
            jax.ShapeDtypeStruct((16, 4, 64, 128), F32),
            jax.ShapeDtypeStruct((12, 2, 48, 128), F32),
            jax.ShapeDtypeStruct((8, 32, 128), F32),
        ],
        scratch_shapes=[pltpu.VMEM((9, 12, 2, 64, 128), F32), pltpu.VMEM((9, 10, 1, 48, 128), F32)],
        compiler_params=pltpu.CompilerParams(vmem_limit_bytes=40 << 20),
    )(charge)


def sweep(dst, src, f, planes, rows, J, lv, kf, kb, f_off, d_off, unroll=2, tables=None):
    first, count = planes
    up, down = tables

    def plane(z, _):
        for row in range(rows[0], rows[0] + rows[1], 8):
            here = pl.ds(row, 8)
            v = [src[z, j, here, :] for j in range(J)]
            left, right = x_down(v, down), x_up(v, up)
            for j in range(J):
                s = (left[j] + right[j]) + (src[z - 1, j, here, :] + src[z + 1, j, here, :])
                s = s + (src[z, j, pl.ds(row - 1, 8), :] + src[z, j, pl.ds(row + 1, 8), :])
                s = kb * (s + lv.r * v[j])
                g = f[z + f_off[0], j, pl.ds(row + f_off[1], 8), :]
                dst[z + d_off[0], j, pl.ds(row + d_off[1], 8), :] = s + (g if kf == 1.0 else kf * g)
        return 0

    lax.fori_loop(first, first + count, plane, 0, unroll=unroll)


NEAR = [(dz, dy) for dz in (-1, 0, 1) for dy in (-1, 0, 1) if (dz, dy) != (0, 0)]
FAR = [(k, dy) for k in range(-4, 5) for dy in (-1, 0, 1) if (k, dy) != (0, 0)]


def pick(d, neg, zero, pos):
    return (zero, pos, neg)[d]


def exchange_kernel(f_ref, s1_ref, s2_ref, b0_ref, q_ref, FX, H1, H2, HB, SX, G1, G2, B1, S2X, U0, U1,
                    Z2, Y2, C2, Z1, Y1, C1, local, sf, rf, s1s, s1r, e1s, e1r, e2s, e2r):
    slab, col = lax.axis_index("slab"), lax.axis_index("col")
    slabs, cols = lax.axis_size("slab"), lax.axis_size("col")
    tables = shift_tables(8)

    def target(o):
        return (lax.rem(slab + o[0] + slabs, slabs), lax.rem(col + o[1] + cols, cols))

    own = pltpu.make_async_copy(f_ref, FX.at[pl.ds(3, 16), :, pl.ds(8, 64), :], local.at[0])
    own.start()
    barrier = pltpu.get_barrier_semaphore()
    for o in FAR:
        pl.semaphore_signal(barrier, inc=1, device_id=target(o), device_id_type=MESH)
    pl.semaphore_wait(barrier, len(FAR))

    def send(src, dst, ss, rs, k, o):
        copy = pltpu.make_async_remote_copy(
            src_ref=src, dst_ref=dst, send_sem=ss.at[k], recv_sem=rs.at[k], device_id=target(o), device_id_type=MESH
        )
        copy.start()
        return copy

    def slot(Z, Y, C, o):
        dz, dy = o
        if dy == 0:
            return Z.at[(dz + 1) // 2]
        if dz == 0:
            return Y.at[(dy + 1) // 2]
        return C.at[(dz + 1) + (dy + 1) // 2]

    first = []
    for k, o in enumerate(NEAR):
        z = pick(o[0], pl.ds(0, 2), pl.ds(2, 4), pl.ds(6, 2))
        y = pick(o[1], pl.ds(0, 8), pl.ds(8, 16), pl.ds(24, 8))
        first.append(send(s2_ref.at[z, y], slot(Z2, Y2, C2, o), e1s, e1r, k, o))
    second = []
    for k, o in enumerate(NEAR):
        z = pick(o[0], pl.ds(1, 5), pl.ds(1, 10), pl.ds(6, 5))
        y = pick(o[1], pl.ds(7, 5), pl.ds(7, 34), pl.ds(36, 5))
        second.append(send(s1_ref.at[z, :, y], slot(Z1, Y1, C1, o), s1s, s1r, k, o))
    own.wait()
    third = []
    for k, o in enumerate(NEAR):
        z = pick(o[0], pl.ds(3, 3), pl.ds(3, 16), pl.ds(16, 3))
        zt = pick(o[0], pl.ds(19, 3), pl.ds(3, 16), pl.ds(0, 3))
        y = pick(o[1], pl.ds(8, 3), pl.ds(8, 64), pl.ds(69, 3))
        yt = pick(o[1], pl.ds(72, 3), pl.ds(8, 64), pl.ds(5, 3))
        third.append(send(FX.at[z, :, y], FX.at[zt, :, yt], sf, rf, k, o))

    mid = S2X.at[pl.ds(13, 4), 0, pl.ds(16, 16)]
    mid[...] = s2_ref[2:6, 8:24, :]
    for copy in first:
        copy.wait_recv()
    for k, o in enumerate(NEAR):
        z = pick(o[0], pl.ds(15, 2), pl.ds(13, 4), pl.ds(13, 2))
        y = pick(o[1], pl.ds(24, 8), pl.ds(16, 16), pl.ds(16, 8))
        S2X[z, 0, y, :] = S2X[z, 0, y, :] + slot(Z2, Y2, C2, o)[...]
    fourth = []
    for k, o in enumerate(FAR):
        d, dy = o
        p0, np_ = (3, 1) if d == 4 else (0, 1) if d == -4 else (0, 4)
        r0, nr = (0, 16) if dy == 0 or abs(d) < 3 else (8, 8) if dy == 1 else (0, 8)
        src = S2X.at[pl.ds(13 + p0, np_), 0, pl.ds(16 + r0, nr)]
        dst = S2X.at[pl.ds(13 + p0 - 4 * d, np_), 0, pl.ds(16 + r0 - 16 * dy, nr)]
        fourth.append(send(src, dst, e2s, e2r, k, o))

    SX[2:14] = s1_ref[...]
    for z in (0, 1, 14, 15):
        SX[z] = jnp.zeros(SX.shape[1:], F32)
    for copy in second:
        copy.wait_recv()
    for k, o in enumerate(NEAR):
        z = pick(o[0], pl.ds(11, 5), pl.ds(3, 10), pl.ds(0, 5))
        y = pick(o[1], pl.ds(39, 5), pl.ds(7, 34), pl.ds(4, 5))
        SX[z, :, y, :] = SX[z, :, y, :] + slot(Z1, Y1, C1, o)[...]
    run = functools.partial(sweep, J=2, lv=L1, tables=tables, f_off=(0, 0))
    run(G1, SX, SX, (1, 14), (5, 40), kf=1.0, kb=L1.b, d_off=(0, 0))
    run(G2, G1, SX, (2, 12), (6, 40), kf=1.0, kb=L1.b, d_off=(0, 0))
    k1 = L0.t * L1.c * SIGMA1
    run(B1, G2, SX, (3, 10), (7, 40), kf=k1, kb=k1 * L1.b, d_off=(-2, 0))

    for copy in third:
        copy.wait_recv()
    run = functools.partial(sweep, J=4, lv=L0, tables=tables, f_off=(0, 0))
    run(H1, FX, FX, (1, 20), (6, 72), kf=1.0, kb=L0.b, d_off=(0, 0))
    run(H2, H1, FX, (2, 18), (7, 72), kf=1.0, kb=L0.b, d_off=(0, 0))
    k0 = FOUR_PI * L0.c
    run(HB, H2, FX, (3, 16), (8, 64), kf=k0, kb=k0 * L0.b, d_off=(-3, -8))
    out = pltpu.make_async_copy(HB, b0_ref, local.at[1])
    out.start()

    for copy in fourth:
        copy.wait_recv()
    src = S2X
    k2 = L0.t * L1.t * L2.c * SIGMA2
    for n in range(1, COARSE_SWEEPS):
        dst = (U0, U1)[n % 2]
        last = n == COARSE_SWEEPS - 1
        rows = 16 + 2 * (13 - n)
        sweep(dst, src, S2X, (n, 30 - 2 * n), (3 + n, -(-rows // 8) * 8), 1, L2, k2 if last else 1.0,
              k2 * L2.b if last else L2.b, (0, 0), (0, 0), tables=tables)
        src = dst

    def children(i, _):
        for y in (-4, 4, 12):
            q = lambda dz, dy: [src[i + 12 + dz, 0, pl.ds(16 + y + dy, 8), :]]
            for (pz, py), kids in prolong_parts(q, L1, *tables).items():
                rows = pl.ds(2 * y + py + 8, 8, stride=2)
                for j, v in enumerate(kids):
                    q_ref[2 * i + pz, j, rows, :] = v + B1[2 * i + pz, j, rows, :]
        return 0

    lax.fori_loop(0, 6, children, 0, unroll=2)

    out.wait()
    for copy in first + second + third + fourth:
        copy.wait_send()


def exchange(f, s1, s2):
    any_, vmem = pl.BlockSpec(memory_space=pl.ANY), pl.BlockSpec(memory_space=pltpu.VMEM)
    big, mid, small = (22, 4, 80, 128), (16, 2, 48, 128), (30, 1, 48, 128)
    shapes = [big, big, big, (16, 4, 64, 128), mid, mid, mid, (12, 2, 48, 128), small, small, small,
              (2, 2, 16, 128), (2, 4, 8, 128), (4, 2, 8, 128), (2, 5, 2, 34, 128), (2, 10, 2, 5, 128), (4, 5, 2, 5, 128)]
    return pl.pallas_call(
        exchange_kernel,
        in_specs=[any_, vmem, vmem],
        out_specs=[any_, vmem],
        out_shape=[jax.ShapeDtypeStruct((16, 4, 64, 128), F32), jax.ShapeDtypeStruct((12, 2, 48, 128), F32)],
        scratch_shapes=[pltpu.VMEM(s, F32) for s in shapes]
        + [pltpu.SemaphoreType.DMA((2,))]
        + [pltpu.SemaphoreType.DMA((n,)) for n in (8, 8, 8, 8, 8, 8, len(FAR), len(FAR))],
        compiler_params=pltpu.CompilerParams(collective_id=0, has_side_effects=True, vmem_limit_bytes=48 << 20),
    )(f, s1, s2)


def fine_kernel(b_ref, q_ref, o_ref, W):
    step = pl.program_id(0)
    planes = b_ref.shape[0]
    tables = shift_tables(8)
    lane = lane_of(8)

    def pair(i, _):
        zc = step * (planes // 2) + i + 2
        for y in range(0, 32, 8):
            q = lambda dz, dy: [q_ref[zc + dz, j, pl.ds(8 + y + dy, 8), :] for j in (0, 1)]
            for (pz, py), kids in prolong_parts(q, L0, *tables).items():
                rows = pl.ds(2 * y + py, 8, stride=2)
                for j, v in enumerate(kids):
                    W[2 * i + pz, j, rows, :] = v + b_ref[2 * i + pz, j, rows, :]
        return 0

    lax.fori_loop(0, planes // 2, pair, 0, unroll=True)

    def reorder(z, _):
        for r in range(0, 64, 8):
            v = [W[z, j, pl.ds(r, 8), :] for j in range(4)]
            for k, w in enumerate(from_groups(v, lane)):
                o_ref[z, pl.ds(r, 8), pl.ds(128 * k, 128)] = w
        return 0

    lax.fori_loop(0, planes, reorder, 0, unroll=2)


def fine(b0, q):
    step = 4
    return pl.pallas_call(
        fine_kernel,
        grid=(16 // step,),
        in_specs=[
            pl.BlockSpec((step, 4, 64, 128), lambda i: (i, 0, 0, 0)),
            pl.BlockSpec((12, 2, 48, 128), lambda i: (0, 0, 0, 0)),
        ],
        out_specs=pl.BlockSpec((step, 64, 512), lambda i: (i, 0, 0)),
        out_shape=jax.ShapeDtypeStruct((16, 64, 512), F32),
        scratch_shapes=[pltpu.VMEM((step, 4, 64, 128), F32)],
        compiler_params=pltpu.CompilerParams(vmem_limit_bytes=24 << 20),
    )(b0, q)


def per_device(charge):
    f, s1, s2 = local_sources(charge)
    b0, q = exchange(f, s1, s2)
    return fine(b0, q)


def solution(mesh):
    placed = (P("slab", "col", None),)
    return jax.shard_map(
        per_device, mesh=mesh, in_specs=placed, out_specs=P("slab", "col", None), check_vma=False
    )
```

profile of v0, /device:TPU:1, one launch (start us, length us, event | category | flops | bytes accessed | tf_op | source)
XLA Modules:
  0.0 46.2 jit_solution(14646262931336706648)
XLA Ops:
  0.0 0.0 copy-start
  0.0 1.6 %copy-done = f32[16,64,512]{2,1,0:T(8,128)S(1)} copy-done((f32[16,64,512]{2,1,0:T(8,128)S(1)}, f32[16,64,512]{2,1,0:T(8,128)}, u32[]{:S(2)}) %copy-start) | copy-done | bytes 2097176
  1.6 3.3 %shard_map.17 = (f32[16,4,64,128]{3,2,1,0:T(8,128)S(1)}, f32[12,2,48,128]{3,2,1,0:T(8,128)S(1)}, f32[8,32,128]{2,1,0:T(8,128)S(1)}) custom-call(f32[16,64,512]{2,1,0:T(8,128)S(1)} %copy-done), custom_call_target="tpu_custom_call" | custom-call | tf_op jit(solution)/shard_map/pallas_call | solution.py:212
  4.9 37.8 %shard_map.18 = (f32[16,4,64,128]{3,2,1,0:T(8,128)S(1)}, f32[12,2,48,128]{3,2,1,0:T(8,128)S(1)}) custom-call(f32[16,4,64,128]{3,2,1,0:T(8,128)S(1)} %get-tuple-element.10.f_ref, f32[12,2,48,128]{3,2,1,0:T(8,128)S(1)} %get-tuple-element.11.s1_ref, f32[8,32,128]{2,1,0:T(8,128)S(1)} %get-tuple-element.12.s2_ref), custom_call_target="tpu_custom_call" | custom-call | tf_op jit(solution)/shard_map/pallas_call | solution.py:384
  42.7 3.4 %shard_map.19 = f32[16,64,512]{2,1,0:T(8,128)} custom-call(f32[16,4,64,128]{3,2,1,0:T(8,128)S(1)} %get-tuple-element.13.b_ref, f32[12,2,48,128]{3,2,1,0:T(8,128)S(1)} %get-tuple-element.14.q_ref), custom_call_target="tpu_custom_call" | custom-call | tf_op jit(solution)/shard_map/pallas_call | solution.py:426
Async XLA Ops:
  0.0 1.6 %copy-start = (f32[16,64,512]{2,1,0:T(8,128)S(1)}, f32[16,64,512]{2,1,0:T(8,128)}, u32[]{:S(2)}) copy-start(f32[16,64,512]{2,1,0:T(8,128)} %x_ref.1) | copy-start | bytes 6291460
where the time goes:
time: 46.3 us; the launch traced here: 46.2 us
  Pallas kernels  44.6 us (96%)
  local copies, waits for them, and re-layouts  1.59 us (3%)
    pallas_call x1, Pallas kernels, exchange(): pl.pallas_call(exchange_kernel, in_specs=[any_, vmem, vmem], out_specs=[a...  37.8 us
    pallas_call x1, Pallas kernels, fine(): pl.pallas_call(fine_kernel, grid=(16 // step,), in_specs=[pl.BlockSpec((s...  3.44 us
    pallas_call x1, Pallas kernels, local_sources(): pl.pallas_call(source_kernel, grid=(16 // step,), in_specs=[pl.BlockSpec(...  3.27 us
    unnamed x2, local copies, waits for them, and re-layouts  1.59 us

commit v1 on v0

v1 whole, which is shorter than its diff:
```python
import functools
import math

import jax
import jax.numpy as jnp
from jax import lax
from jax.experimental import pallas as pl
from jax.experimental.pallas import tpu as pltpu
from jax.sharding import PartitionSpec as P

COARSE_SWEEPS = 12
KAPPA = 0.001
OMEGA = 0.8
FOUR_PI = 12.566370614359172
MESH = pl.DeviceIdType.MESH
F32 = jnp.float32


class Level:
    def __init__(self, scale):
        self.c = OMEGA / (6.0 * scale + KAPPA)
        self.a = 1.0 - OMEGA
        self.b = self.c * scale
        self.r = self.a / self.b
        self.t = 2.0 * self.b * self.b
        self.rho = self.r + 2.0
        self.alpha = (self.a**2 + 6.0 * self.a * self.b + 12.0 * self.b**2) / self.t


L0, L1, L2 = Level(1.0), Level(0.25), Level(0.0625)
SIGMA1 = FOUR_PI * L0.t / 8.0
SIGMA2 = SIGMA1 * L1.t / 8.0


def lane_of(n):
    return lax.broadcasted_iota(jnp.int32, (n, 128), 1)


def take(v, idx):
    return jnp.take_along_axis(v, idx, axis=1, mode="promise_in_bounds")


def shift_tables(n):
    lane = lane_of(n)
    up = jnp.where(lane < 124, lane + 4, (lane + 1) % 4)
    down = jnp.where(lane < 4, 124 + (lane + 3) % 4, lane - 4)
    return up, down


def x_up(v, up):
    return v[1:] + [take(v[0], up)]


def x_down(v, down):
    return [take(v[-1], down)] + v[:-1]


def swap(p, q, bit, lane):
    clear = (lane & bit) == 0
    t = take(jnp.where(clear, q, p), lane ^ bit)
    return jnp.where(clear, p, t), jnp.where(clear, t, q)


def to_groups(v, lane):
    a0, a1 = swap(v[0], v[1], 1, lane)
    a2, a3 = swap(v[2], v[3], 1, lane)
    b0, b2 = swap(a0, a2, 2, lane)
    b1, b3 = swap(a1, a3, 2, lane)
    return [b0, b1, b2, b3]


def from_groups(v, lane):
    b0, b2 = swap(v[0], v[2], 2, lane)
    b1, b3 = swap(v[1], v[3], 2, lane)
    a0, a1 = swap(b0, b1, 1, lane)
    a2, a3 = swap(b2, b3, 1, lane)
    return [a0, a1, a2, a3]


def fourier_tables():
    lane, mode = lax.broadcasted_iota(jnp.int32, (128, 128), 0), lax.broadcasted_iota(jnp.int32, (128, 128), 1)
    cell = 32 * (lane % 4) + lane // 4
    freq = jnp.where(mode <= 64, mode, mode - 64)
    turn = (cell * freq + jnp.where(mode <= 64, 0, 96)) % 128
    single = (mode == 0) | (mode == 64)
    norm = jnp.where(single, math.sqrt(1.0 / 128.0), math.sqrt(2.0 / 128.0)).astype(F32)
    basis = norm * jnp.cos((2.0 * math.pi / 128.0) * turn.astype(F32))
    eigen = 2.0 * jnp.cos((2.0 * math.pi / 128.0) * freq[0:8].astype(F32)) + L2.r
    return basis, eigen


def transform(v, basis, dims):
    return lax.dot_general(v, basis, ((((1,), (dims,))), ((), ())), precision=lax.Precision.HIGHEST,
                           preferred_element_type=F32)


def add(*lists):
    out = lists[0]
    for l in lists[1:]:
        out = [a + b for a, b in zip(out, l)]
    return out


def mul(k, v):
    return [k * a for a in v]


def restrict_parts(load, lv, up, down):
    E, V = {}, {}
    for pz in (0, 1):
        for py in (0, 1):
            lo, hi = load(pz, py)
            E[pz, py] = add(lo, hi)
            V[pz, py] = add(x_up(lo, up), x_down(hi, down))
    K = {k: add(mul(lv.rho, E[k]), V[k]) for k in E}
    p = add(E[0, 0], E[0, 1], E[1, 0], E[1, 1])
    hp = mul(0.5, p)
    n0 = add(mul(lv.alpha, p), x_up(hp, up), x_down(hp, down))
    n0 = add(n0, mul(lv.rho, add(V[0, 0], V[0, 1], V[1, 0], V[1, 1])))
    nu = add(hp, K[0, 0], K[1, 0])
    nd = add(hp, K[0, 1], K[1, 1])
    zu = add(hp, K[0, 0], K[0, 1])
    zd = add(hp, K[1, 0], K[1, 1])
    return [n0, nu, nd, zu, E[0, 0], E[0, 1], zd, E[1, 0], E[1, 1]]


def gather_parts(T, z, j, row, n):
    here, above, below = pl.ds(row, n), pl.ds(row + 1, n), pl.ds(row - 1, n)
    out = T[0, z, j, here, :] + T[3, z + 1, j, here, :] + T[6, z - 1, j, here, :]
    out = out + (T[1, z, j, above, :] + T[4, z + 1, j, above, :] + T[7, z - 1, j, above, :])
    return out + (T[2, z, j, below, :] + T[5, z + 1, j, below, :] + T[8, z - 1, j, below, :])


def prolong_parts(q, lv, up, down):
    c = q(0, 0)
    zs, ys = (q(-1, 0), q(1, 0)), (q(0, -1), q(0, 1))
    n = add(zs[0], zs[1], ys[0], ys[1], x_up(c, up), x_down(c, down))
    n = add(mul(lv.alpha, c), mul(0.5, n))
    rc = mul(lv.rho, c)
    out = {}
    for pz in (0, 1):
        for py in (0, 1):
            s = add(zs[pz], ys[py])
            w = add(rc, s)
            A = add(n, mul(lv.rho, s), q(2 * pz - 1, 2 * py - 1))
            lo, hi = add(A, x_down(w, down)), add(A, x_up(w, up))
            out[pz, py] = [v for pair in zip(lo, hi) for v in pair]
    return out


CHUNK = 2


def chunk_at(i):
    return (i % 2) * (16 // CHUNK - 1 - i // 2) + (1 - i % 2) * (i // 2)


def local_sources(X, arrived, met, FX, s1_ref, s2_ref, T0, T1):
    lane = lane_of(8)
    up, down = shift_tables(8)

    def clear(i, _):
        for z in (0, 1, 10, 11):
            T0[i, z] = jnp.zeros((2, 64, 128), F32)
        for z in range(2, 10):
            T0[i, z, :, 0:16, :] = jnp.zeros((2, 16, 128), F32)
            T0[i, z, :, 48:64, :] = jnp.zeros((2, 16, 128), F32)
        T1[i] = jnp.zeros(T1.shape[1:], F32)
        return 0

    lax.fori_loop(0, 9, clear, 0)
    s1_ref[0] = jnp.zeros(s1_ref.shape[1:], F32)
    s1_ref[11] = jnp.zeros(s1_ref.shape[1:], F32)

    def chunk(i, _):
        c = chunk_at(i)
        arrived(c)
        for i in range(CHUNK):
            z = c * CHUNK + i
            for r in range(0, 64, 8):
                v = [X[z, pl.ds(r, 8), pl.ds(128 * k, 128)] for k in range(4)]
                for j, w in enumerate(to_groups(v, lane)):
                    FX[z + 3, j, pl.ds(8 + r, 8), :] = w
        for i in range(CHUNK // 2):
            zc = c * (CHUNK // 2) + i
            for y in range(0, 32, 8):

                def load(pz, py):
                    rows = pl.ds(8 + 2 * y + py, 8, stride=2)
                    v = [FX[2 * zc + pz + 3, j, rows, :] for j in range(4)]
                    return v[0::2], v[1::2]

                for k, part in enumerate(restrict_parts(load, L0, up, down)):
                    for j, v in enumerate(part):
                        T0[k, zc + 2, j, pl.ds(16 + y, 8), :] = v
        return 0

    lax.fori_loop(0, 4, chunk, 0)
    met()
    lax.fori_loop(4, 16 // CHUNK, chunk, 0)

    def sums0(z, _):
        for j in (0, 1):
            for r in range(0, 48, 8):
                s1_ref[z, j, pl.ds(r, 8), :] = gather_parts(T0, z, j, r + 8, 8)
        return 0

    lax.fori_loop(1, 11, sums0, 0, unroll=2)

    def parts1(i, _):
        for y in (-4, 4, 12):

            def load(pz, py):
                rows = pl.ds(2 * y + py + 8, 8, stride=2)
                v = [s1_ref[2 * i + pz, j, rows, :] for j in (0, 1)]
                return v[0:1], v[1:2]

            for k, part in enumerate(restrict_parts(load, L1, up, down)):
                T1[k, i + 2, 0, pl.ds(16 + y, 8), :] = part[0]
        return 0

    lax.fori_loop(0, 6, parts1, 0, unroll=True)

    def sums1(z, _):
        for r in range(0, 32, 8):
            s2_ref[z, pl.ds(r, 8), :] = gather_parts(T1, z + 1, 0, r + 8, 8)
        return 0

    lax.fori_loop(0, 8, sums1, 0, unroll=2)


def sweep(dst, src, f, planes, rows, J, lv, kf, kb, f_off, d_off, unroll=2, tables=None):
    first, count = planes
    up, down = tables

    def plane(z, _):
        for row in range(rows[0], rows[0] + rows[1], 8):
            here = pl.ds(row, 8)
            v = [src[z, j, here, :] for j in range(J)]
            left, right = x_down(v, down), x_up(v, up)
            for j in range(J):
                s = (left[j] + right[j]) + (src[z - 1, j, here, :] + src[z + 1, j, here, :])
                s = s + (src[z, j, pl.ds(row - 1, 8), :] + src[z, j, pl.ds(row + 1, 8), :])
                s = kb * (s + lv.r * v[j])
                g = f[z + f_off[0], j, pl.ds(row + f_off[1], 8), :]
                dst[z + d_off[0], j, pl.ds(row + d_off[1], 8), :] = s + (g if kf == 1.0 else kf * g)
        return 0

    lax.fori_loop(first, first + count, plane, 0, unroll=unroll)


def modal_sweep(dst, src, f, eigen, planes, rows, kf, kb):
    eig = eigen[...]

    def plane(z, _):
        for row in range(rows[0], rows[0] + rows[1], 8):
            here = pl.ds(row, 8)
            s = src[z - 1, 0, here, :] + src[z + 1, 0, here, :]
            s = s + (src[z, 0, pl.ds(row - 1, 8), :] + src[z, 0, pl.ds(row + 1, 8), :])
            g = f[z, 0, here, :]
            dst[z, 0, here, :] = kb * (s + eig * src[z, 0, here, :]) + (g if kf == 1.0 else kf * g)
        return 0

    lax.fori_loop(planes[0], planes[0] + planes[1], plane, 0, unroll=4)


NEAR = [(dz, dy) for dz in (-1, 0, 1) for dy in (-1, 0, 1) if (dz, dy) != (0, 0)]
FAR = [(k, dy) for k in range(-4, 5) for dy in (-1, 0, 1) if (k, dy) != (0, 0)]


def pick(d, neg, zero, pos):
    return (zero, pos, neg)[d]


def exchange_kernel(x_ref, b0_ref, q_ref, basis, eigen, X, T0, T1, s1_ref, s2_ref, FX, H1, H2, SX, G1, G2, B1, S2X, U0, U1,
                    Z2, Y2, C2, Z1, Y1, C1, load_sem, sf, rf, s1s, s1r, e1s, e1r, e2s, e2r):
    slab, col = lax.axis_index("slab"), lax.axis_index("col")
    slabs, cols = lax.axis_size("slab"), lax.axis_size("col")
    tables = shift_tables(8)

    def target(o):
        return (lax.rem(slab + o[0] + slabs, slabs), lax.rem(col + o[1] + cols, cols))

    def fetch(c):
        part = pl.ds(c * CHUNK, CHUNK)
        return pltpu.make_async_copy(x_ref.at[part], X.at[part], load_sem.at[c])

    for i in range(16 // CHUNK):
        fetch(chunk_at(i)).start()
    barrier = pltpu.get_barrier_semaphore()
    for o in FAR:
        pl.semaphore_signal(barrier, inc=1, device_id=target(o), device_id_type=MESH)
    def send(src, dst, ss, rs, k, o):
        copy = pltpu.make_async_remote_copy(
            src_ref=src, dst_ref=dst, send_sem=ss.at[k], recv_sem=rs.at[k], device_id=target(o), device_id_type=MESH
        )
        copy.start()
        return copy

    third = []

    full = (8, 8, 64)
    along_z = [((1, 0), (17, 1, 2), full), ((-1, 0), (3, 19, 2), full)]
    outer = [((1, 0), (16, 0, 1), full), ((-1, 0), (5, 21, 1), full)]
    rest = []
    for dy, rows in ((1, (69, 5, 3)), (-1, (8, 72, 3))):
        rest += [((0, dy), (3, 3, 16), rows), ((1, dy), (16, 0, 3), rows), ((-1, dy), (3, 19, 3), rows)]

    def fine_layers(pieces):
        for o, (z, zt, nz), (y, yt, ny) in pieces:
            src = FX.at[pl.ds(z, nz), :, pl.ds(y, ny)]
            third.append(send(src, FX.at[pl.ds(zt, nz), :, pl.ds(yt, ny)], sf, rf, len(third), o))

    def met():
        pl.semaphore_wait(barrier, len(FAR))
        fine_layers(along_z)

    local_sources(X, lambda c: fetch(c).wait(), met, FX, s1_ref, s2_ref, T0, T1)

    def slot(Z, Y, C, o):
        dz, dy = o
        if dy == 0:
            return Z.at[(dz + 1) // 2]
        if dz == 0:
            return Y.at[(dy + 1) // 2]
        return C.at[(dz + 1) + (dy + 1) // 2]

    first = []
    for k, o in enumerate(NEAR):
        z = pick(o[0], pl.ds(0, 2), pl.ds(2, 4), pl.ds(6, 2))
        y = pick(o[1], pl.ds(0, 8), pl.ds(8, 16), pl.ds(24, 8))
        first.append(send(s2_ref.at[z, y], slot(Z2, Y2, C2, o), e1s, e1r, k, o))
    second = []
    for k, o in enumerate(NEAR):
        z = pick(o[0], pl.ds(1, 5), pl.ds(1, 10), pl.ds(6, 5))
        y = pick(o[1], pl.ds(7, 5), pl.ds(7, 34), pl.ds(36, 5))
        second.append(send(s1_ref.at[z, :, y], slot(Z1, Y1, C1, o), s1s, s1r, k, o))
    fine_layers(rest)

    fine_layers(outer)
    mid = S2X.at[pl.ds(13, 4), 0, pl.ds(16, 16)]
    mid[...] = s2_ref[2:6, 8:24, :]
    basis[...], eigen[...] = fourier_tables()
    for copy in first:
        copy.wait_recv()
    for k, o in enumerate(NEAR):
        z = pick(o[0], pl.ds(15, 2), pl.ds(13, 4), pl.ds(13, 2))
        y = pick(o[1], pl.ds(24, 8), pl.ds(16, 16), pl.ds(16, 8))
        S2X[z, 0, y, :] = S2X[z, 0, y, :] + slot(Z2, Y2, C2, o)[...]
    S2X[13:17, 0, 16:32, :] = transform(mid[...].reshape(64, 128), basis[...], 0).reshape(4, 16, 128)
    fourth = []
    for k, o in enumerate(FAR):
        d, dy = o
        p0, np_ = (3, 1) if d == 4 else (0, 1) if d == -4 else (0, 4)
        nr = 16 if dy == 0 else (13, 13, 9, 5, 1)[abs(d)]
        r0 = 16 - nr if dy == 1 else 0
        src = S2X.at[pl.ds(13 + p0, np_), 0, pl.ds(16 + r0, nr)]
        dst = S2X.at[pl.ds(13 + p0 - 4 * d, np_), 0, pl.ds(16 + r0 - 16 * dy, nr)]
        fourth.append(send(src, dst, e2s, e2r, k, o))

    SX[2:14] = s1_ref[...]
    for z in (0, 1, 14, 15):
        SX[z] = jnp.zeros(SX.shape[1:], F32)
    for copy in second:
        copy.wait_recv()
    for k, o in enumerate(NEAR):
        z = pick(o[0], pl.ds(11, 5), pl.ds(3, 10), pl.ds(0, 5))
        y = pick(o[1], pl.ds(39, 5), pl.ds(7, 34), pl.ds(4, 5))
        SX[z, :, y, :] = SX[z, :, y, :] + slot(Z1, Y1, C1, o)[...]
    run = functools.partial(sweep, J=2, lv=L1, tables=tables, f_off=(0, 0))
    run(G1, SX, SX, (1, 14), (5, 40), kf=1.0, kb=L1.b, d_off=(0, 0))
    run(G2, G1, SX, (2, 12), (6, 40), kf=1.0, kb=L1.b, d_off=(0, 0))
    k1 = L0.t * L1.c * SIGMA1
    run(B1, G2, SX, (3, 10), (7, 40), kf=k1, kb=k1 * L1.b, d_off=(-2, 0))

    for copy in third:
        copy.wait_recv()
    run = functools.partial(sweep, J=4, lv=L0, tables=tables, f_off=(0, 0))
    run(H1, FX, FX, (1, 20), (6, 72), kf=1.0, kb=L0.b, d_off=(0, 0))
    run(H2, H1, FX, (2, 18), (7, 72), kf=1.0, kb=L0.b, d_off=(0, 0))
    k0 = FOUR_PI * L0.c
    run(b0_ref, H2, FX, (3, 16), (8, 64), kf=k0, kb=k0 * L0.b, d_off=(-3, -8))

    for copy in fourth:
        copy.wait_recv()
    src = S2X
    k2 = L0.t * L1.t * L2.c * SIGMA2
    for n in range(1, COARSE_SWEEPS):
        dst = (U0, U1)[n % 2]
        last = n == COARSE_SWEEPS - 1
        rows = 16 + 2 * (13 - n)
        kf, kb = (k2, k2 * L2.b) if last else (1.0, L2.b)
        modal_sweep(dst, src, S2X, eigen, (n, 30 - 2 * n), (3 + n, rows), kf, kb)
        src = dst
    U0[11:19, 0, 12:36, :] = transform(src[11:19, 0, 12:36, :].reshape(192, 128), basis[...], 1).reshape(8, 24, 128)
    src = U0

    def children(i, _):
        for y in (-4, 4, 12):
            q = lambda dz, dy: [src[i + 12 + dz, 0, pl.ds(16 + y + dy, 8), :]]
            for (pz, py), kids in prolong_parts(q, L1, *tables).items():
                rows = pl.ds(2 * y + py + 8, 8, stride=2)
                for j, v in enumerate(kids):
                    q_ref[2 * i + pz, j, rows, :] = v + B1[2 * i + pz, j, rows, :]
        return 0

    lax.fori_loop(0, 6, children, 0, unroll=2)

    for copy in first + second + third + fourth:
        copy.wait_send()


def exchange(charge):
    hbm, vmem = pl.BlockSpec(memory_space=pltpu.HBM), pl.BlockSpec(memory_space=pltpu.VMEM)
    big, mid, small = (22, 4, 80, 128), (16, 2, 48, 128), (30, 1, 48, 128)
    shapes = [(128, 128), (8, 128), (16, 64, 512), (9, 12, 2, 64, 128), (9, 10, 1, 48, 128), (12, 2, 48, 128), (8, 32, 128), big, big, big, mid, mid, mid, (12, 2, 48, 128), small, small, small,
              (2, 2, 16, 128), (2, 4, 8, 128), (4, 2, 8, 128), (2, 5, 2, 34, 128), (2, 10, 2, 5, 128), (4, 5, 2, 5, 128)]
    return pl.pallas_call(
        exchange_kernel,
        in_specs=[hbm],
        out_specs=[vmem, vmem],
        out_shape=[jax.ShapeDtypeStruct((16, 4, 64, 128), F32), jax.ShapeDtypeStruct((12, 2, 48, 128), F32)],
        scratch_shapes=[pltpu.VMEM(s, F32) for s in shapes]
        + [pltpu.SemaphoreType.DMA((16 // CHUNK,))]
        + [pltpu.SemaphoreType.DMA((n,)) for n in (10, 10, 8, 8, 8, 8, len(FAR), len(FAR))],
        compiler_params=pltpu.CompilerParams(collective_id=0, has_side_effects=True, vmem_limit_bytes=48 << 20),
    )(pltpu.with_memory_space_constraint(charge, pltpu.HBM))


def fine_kernel(b_ref, q_ref, o_ref, W, O, sems):
    tables = shift_tables(8)
    lane = lane_of(8)

    def store(i):
        part = pl.ds(i * CHUNK, CHUNK)
        return pltpu.make_async_copy(O.at[part], o_ref.at[part], sems.at[i])

    def pair(i, _):
        for y in range(0, 32, 8):
            q = lambda dz, dy: [q_ref[i + 2 + dz, j, pl.ds(8 + y + dy, 8), :] for j in (0, 1)]
            for (pz, py), kids in prolong_parts(q, L0, *tables).items():
                rows = pl.ds(2 * y + py, 8, stride=2)
                for j, v in enumerate(kids):
                    W[2 * i + pz, j, rows, :] = v + b_ref[2 * i + pz, j, rows, :]
        for z in range(2):
            for r in range(0, 64, 8):
                v = [W[2 * i + z, j, pl.ds(r, 8), :] for j in range(4)]
                for k, w in enumerate(from_groups(v, lane)):
                    O[2 * i + z, pl.ds(r, 8), pl.ds(128 * k, 128)] = w
        store(i).start()
        return 0

    lax.fori_loop(0, 8, pair, 0)
    for i in range(8):
        store(i).wait()


def fine(b0, q):
    vmem = pl.BlockSpec(memory_space=pltpu.VMEM)
    return pl.pallas_call(
        fine_kernel,
        in_specs=[vmem, vmem],
        out_specs=pl.BlockSpec(memory_space=pl.ANY),
        out_shape=jax.ShapeDtypeStruct((16, 64, 512), F32),
        scratch_shapes=[
            pltpu.VMEM((16, 4, 64, 128), F32),
            pltpu.VMEM((16, 64, 512), F32),
            pltpu.SemaphoreType.DMA((8,)),
        ],
        compiler_params=pltpu.CompilerParams(vmem_limit_bytes=24 << 20),
    )(b0, q)


def per_device(charge):
    b0, q = exchange(charge)
    return fine(b0, q)


def solution(mesh):
    placed = (P("slab", "col", None),)
    return jax.shard_map(
        per_device, mesh=mesh, in_specs=placed, out_specs=P("slab", "col", None), check_vma=False
    )
```

time: 46.3 us -> 32.3 us (0.70)
  Pallas kernels: 44.6 us -> 32.1 us
  local copies, waits for them, and re-layouts: 1.59 us -> 0 us
    pallas_call x3 -> x2, Pallas kernels: 44.6 us -> 32.1 us  [the longest x1 28.8 us: exchange(): pl.pallas_call(exchange_kernel, in_specs=[hbm], out_specs=[vmem, vmem], o...]
    unnamed x2 -> x0, local copies, waits for them, and re-layouts: 1.59 us -> none
where the time goes in v1:
time: 32.3 us; the launch traced here: 32.2 us
  Pallas kernels  32.1 us (99%)
    pallas_call x1, Pallas kernels, exchange(): pl.pallas_call(exchange_kernel, in_specs=[hbm], out_specs=[vmem, vmem], o...  28.8 us
    pallas_call x1, Pallas kernels, fine(): pl.pallas_call(fine_kernel, in_specs=[vmem, vmem], out_specs=pl.BlockSpec...  3.36 us

profile of v1, /device:TPU:1, one launch (start us, length us, event | category | flops | bytes accessed | tf_op | source)
XLA Modules:
  0.0 32.2 jit_solution(16191016251459566746)
XLA Ops:
  0.0 28.8 %shard_map.17 = (f32[16,4,64,128]{3,2,1,0:T(8,128)S(1)}, f32[12,2,48,128]{3,2,1,0:T(8,128)S(1)}) custom-call(f32[16,64,512]{2,1,0:T(8,128)} %x_ref.1), custom_call_target="tpu_custom_call" | custom-call | tf_op jit(solution)/shard_map/pallas_call | solution.py:418
  28.8 3.4 %shard_map.18 = f32[16,64,512]{2,1,0:T(8,128)} custom-call(f32[16,4,64,128]{3,2,1,0:T(8,128)S(1)} %get-tuple-element.7.b_ref, f32[12,2,48,128]{3,2,1,0:T(8,128)S(1)} %get-tuple-element.8.q_ref), custom_call_target="tpu_custom_call" | custom-call | tf_op jit(solution)/shard_map/pallas_call | solution.py:460

commit v2 on v1

--- a/solution.py
+++ b/solution.py
@@ -55,26 +55,17 @@
     return [take(v[-1], down)] + v[:-1]
 
 
-def swap(p, q, bit, lane):
-    clear = (lane & bit) == 0
-    t = take(jnp.where(clear, q, p), lane ^ bit)
-    return jnp.where(clear, p, t), jnp.where(clear, t, q)
-
-
-def to_groups(v, lane):
-    a0, a1 = swap(v[0], v[1], 1, lane)
-    a2, a3 = swap(v[2], v[3], 1, lane)
-    b0, b2 = swap(a0, a2, 2, lane)
-    b1, b3 = swap(a1, a3, 2, lane)
-    return [b0, b1, b2, b3]
-
-
-def from_groups(v, lane):
-    b0, b2 = swap(v[0], v[2], 2, lane)
-    b1, b3 = swap(v[1], v[3], 2, lane)
-    a0, a1 = swap(b0, b1, 1, lane)
-    a2, a3 = swap(b2, b3, 1, lane)
-    return [a0, a1, a2, a3]
+def turn(v, lane):
+    odd, high = (lane & 1) != 0, (lane & 2) != 0
+    a = [jnp.where(odd, v[(d + 1) % 4], v[d]) for d in range(4)]
+    return [jnp.where(high, a[(d + 2) % 4], a[d]) for d in range(4)]
+
+
+def regroup(v, lane):
+    v = turn(v, lane)
+    v = v[:1] + [take(v[d], (lane & 124) | ((lane - d) & 3)) for d in (1, 2, 3)]
+    v = turn(v, lane)
+    return [v[0], v[3], v[2], v[1]]
 
 
 def fourier_tables():
@@ -106,22 +97,21 @@
 
 
 def restrict_parts(load, lv, up, down):
-    E, V = {}, {}
-    for pz in (0, 1):
-        for py in (0, 1):
-            lo, hi = load(pz, py)
-            E[pz, py] = add(lo, hi)
-            V[pz, py] = add(x_up(lo, up), x_down(hi, down))
-    K = {k: add(mul(lv.rho, E[k]), V[k]) for k in E}
+    E, lo, hi = {}, {}, {}
+    for k in ((0, 0), (0, 1), (1, 0), (1, 1)):
+        lo[k], hi[k] = load(*k)
+        E[k] = add(lo[k], hi[k])
+
+    def pair(k, m):
+        return add(mul(lv.rho, add(E[k], E[m])), x_up(add(lo[k], lo[m]), up), x_down(add(hi[k], hi[m]), down))
+
+    z0, z1, y0 = pair((0, 0), (0, 1)), pair((1, 0), (1, 1)), pair((0, 0), (1, 0))
+    total = add(z0, z1)
+    y1 = [a - b for a, b in zip(total, y0)]
     p = add(E[0, 0], E[0, 1], E[1, 0], E[1, 1])
     hp = mul(0.5, p)
-    n0 = add(mul(lv.alpha, p), x_up(hp, up), x_down(hp, down))
-    n0 = add(n0, mul(lv.rho, add(V[0, 0], V[0, 1], V[1, 0], V[1, 1])))
-    nu = add(hp, K[0, 0], K[1, 0])
-    nd = add(hp, K[0, 1], K[1, 1])
-    zu = add(hp, K[0, 0], K[0, 1])
-    zd = add(hp, K[1, 0], K[1, 1])
-    return [n0, nu, nd, zu, E[0, 0], E[0, 1], zd, E[1, 0], E[1, 1]]
+    n0 = add(mul(lv.alpha - lv.rho * lv.rho, p), x_up(hp, up), x_down(hp, down), mul(lv.rho, total))
+    return [n0, add(hp, y0), add(hp, y1), add(hp, z0), E[0, 0], E[0, 1], add(hp, z1), E[1, 0], E[1, 1]]
 
 
 def gather_parts(T, z, j, row, n):
@@ -137,14 +127,16 @@
     n = add(zs[0], zs[1], ys[0], ys[1], x_up(c, up), x_down(c, down))
     n = add(mul(lv.alpha, c), mul(0.5, n))
     rc = mul(lv.rho, c)
+    w = {k: add(rc, zs[k[0]], ys[k[1]]) for k in ((0, 0), (0, 1), (1, 0))}
+    lo = {k: x_down(v, down) for k, v in w.items()}
+    hi = {k: x_up(v, up) for k, v in w.items()}
+    for d in (lo, hi):
+        d[1, 1] = [a + b - c for a, b, c in zip(d[0, 1], d[1, 0], d[0, 0])]
     out = {}
     for pz in (0, 1):
         for py in (0, 1):
-            s = add(zs[pz], ys[py])
-            w = add(rc, s)
-            A = add(n, mul(lv.rho, s), q(2 * pz - 1, 2 * py - 1))
-            lo, hi = add(A, x_down(w, down)), add(A, x_up(w, up))
-            out[pz, py] = [v for pair in zip(lo, hi) for v in pair]
+            A = add(n, mul(lv.rho, add(zs[pz], ys[py])), q(2 * pz - 1, 2 * py - 1))
+            out[pz, py] = [v for pair in zip(add(A, lo[pz, py]), add(A, hi[pz, py])) for v in pair]
     return out
 
 
@@ -179,7 +171,7 @@
             z = c * CHUNK + i
             for r in range(0, 64, 8):
                 v = [X[z, pl.ds(r, 8), pl.ds(128 * k, 128)] for k in range(4)]
-                for j, w in enumerate(to_groups(v, lane)):
+                for j, w in enumerate(regroup(v, lane)):
                     FX[z + 3, j, pl.ds(8 + r, 8), :] = w
         for i in range(CHUNK // 2):
             zc = c * (CHUNK // 2) + i
@@ -195,9 +187,9 @@
                         T0[k, zc + 2, j, pl.ds(16 + y, 8), :] = v
         return 0
 
-    lax.fori_loop(0, 4, chunk, 0)
+    lax.fori_loop(0, 2, chunk, 0)
     met()
-    lax.fori_loop(4, 16 // CHUNK, chunk, 0)
+    lax.fori_loop(2, 16 // CHUNK, chunk, 0)
 
     def sums0(z, _):
         for j in (0, 1):
@@ -265,7 +257,7 @@
 
 
 NEAR = [(dz, dy) for dz in (-1, 0, 1) for dy in (-1, 0, 1) if (dz, dy) != (0, 0)]
-FAR = [(k, dy) for k in range(-4, 5) for dy in (-1, 0, 1) if (k, dy) != (0, 0)]
+FAR = [(s * k, dy) for k in (4, 3, 2, 1, 0) for dy in (-1, 1, 0) for s in (1, -1) if (k, dy) != (0, 0) and (k or s == 1)]
 
 
 def pick(d, neg, zero, pos):
@@ -273,7 +265,7 @@
 
 
 def exchange_kernel(x_ref, b0_ref, q_ref, basis, eigen, X, T0, T1, s1_ref, s2_ref, FX, H1, H2, SX, G1, G2, B1, S2X, U0, U1,
-                    Z2, Y2, C2, Z1, Y1, C1, load_sem, sf, rf, s1s, s1r, e1s, e1r, e2s, e2r):
+                    Z2, Y2, C2, Z1, Y1, C1, load_sem, here, sf, rf, s1s, s1r, e1s, e1r, e2s, e2r):
     slab, col = lax.axis_index("slab"), lax.axis_index("col")
     slabs, cols = lax.axis_size("slab"), lax.axis_size("col")
     tables = shift_tables(8)
@@ -288,7 +280,7 @@
     for i in range(16 // CHUNK):
         fetch(chunk_at(i)).start()
     barrier = pltpu.get_barrier_semaphore()
-    for o in FAR:
+    for o in NEAR:
         pl.semaphore_signal(barrier, inc=1, device_id=target(o), device_id_type=MESH)
     def send(src, dst, ss, rs, k, o):
         copy = pltpu.make_async_remote_copy(
@@ -302,18 +294,28 @@
     full = (8, 8, 64)
     along_z = [((1, 0), (17, 1, 2), full), ((-1, 0), (3, 19, 2), full)]
     outer = [((1, 0), (16, 0, 1), full), ((-1, 0), (5, 21, 1), full)]
-    rest = []
+    across, middle = [], []
     for dy, rows in ((1, (69, 5, 3)), (-1, (8, 72, 3))):
-        rest += [((0, dy), (3, 3, 16), rows), ((1, dy), (16, 0, 3), rows), ((-1, dy), (3, 19, 3), rows)]
+        across += [((1, dy), (16, 0, 3), rows), ((-1, dy), (3, 19, 3), rows)]
+        across += [((0, dy), (3, 3, 4), rows), ((0, dy), (15, 15, 4), rows)]
+        middle += [((0, dy), (7, 7, 8), rows)]
 
     def fine_layers(pieces):
         for o, (z, zt, nz), (y, yt, ny) in pieces:
             src = FX.at[pl.ds(z, nz), :, pl.ds(y, ny)]
             third.append(send(src, FX.at[pl.ds(zt, nz), :, pl.ds(yt, ny)], sf, rf, len(third), o))
 
+    def tell(k):
+        for o in ((k + 1, 0), (-k - 1, 0)):
+            pl.semaphore_signal(here.at[k], inc=1, device_id=target(o), device_id_type=MESH)
+
+    def heard(k):
+        pl.semaphore_wait(here.at[k], 2)
+
     def met():
-        pl.semaphore_wait(barrier, len(FAR))
+        pl.semaphore_wait(barrier, len(NEAR))
         fine_layers(along_z)
+        tell(0)
 
     local_sources(X, lambda c: fetch(c).wait(), met, FX, s1_ref, s2_ref, T0, T1)
 
@@ -328,26 +330,29 @@
     first = []
     for k, o in enumerate(NEAR):
         z = pick(o[0], pl.ds(0, 2), pl.ds(2, 4), pl.ds(6, 2))
-        y = pick(o[1], pl.ds(0, 8), pl.ds(8, 16), pl.ds(24, 8))
+        y = pick(o[1], pl.ds(6, 2), pl.ds(8, 16), pl.ds(24, 2))
         first.append(send(s2_ref.at[z, y], slot(Z2, Y2, C2, o), e1s, e1r, k, o))
     second = []
     for k, o in enumerate(NEAR):
         z = pick(o[0], pl.ds(1, 5), pl.ds(1, 10), pl.ds(6, 5))
         y = pick(o[1], pl.ds(7, 5), pl.ds(7, 34), pl.ds(36, 5))
         second.append(send(s1_ref.at[z, :, y], slot(Z1, Y1, C1, o), s1s, s1r, k, o))
-    fine_layers(rest)
+    fine_layers(middle + across)
 
     fine_layers(outer)
     mid = S2X.at[pl.ds(13, 4), 0, pl.ds(16, 16)]
     mid[...] = s2_ref[2:6, 8:24, :]
+    heard(0)
+    tell(1)
     basis[...], eigen[...] = fourier_tables()
     for copy in first:
         copy.wait_recv()
     for k, o in enumerate(NEAR):
         z = pick(o[0], pl.ds(15, 2), pl.ds(13, 4), pl.ds(13, 2))
-        y = pick(o[1], pl.ds(24, 8), pl.ds(16, 16), pl.ds(16, 8))
+        y = pick(o[1], pl.ds(30, 2), pl.ds(16, 16), pl.ds(16, 2))
         S2X[z, 0, y, :] = S2X[z, 0, y, :] + slot(Z2, Y2, C2, o)[...]
     S2X[13:17, 0, 16:32, :] = transform(mid[...].reshape(64, 128), basis[...], 0).reshape(4, 16, 128)
+    heard(1)
     fourth = []
     for k, o in enumerate(FAR):
         d, dy = o
@@ -414,15 +419,15 @@
     hbm, vmem = pl.BlockSpec(memory_space=pltpu.HBM), pl.BlockSpec(memory_space=pltpu.VMEM)
     big, mid, small = (22, 4, 80, 128), (16, 2, 48, 128), (30, 1, 48, 128)
     shapes = [(128, 128), (8, 128), (16, 64, 512), (9, 12, 2, 64, 128), (9, 10, 1, 48, 128), (12, 2, 48, 128), (8, 32, 128), big, big, big, mid, mid, mid, (12, 2, 48, 128), small, small, small,
-              (2, 2, 16, 128), (2, 4, 8, 128), (4, 2, 8, 128), (2, 5, 2, 34, 128), (2, 10, 2, 5, 128), (4, 5, 2, 5, 128)]
+              (2, 2, 16, 128), (2, 4, 2, 128), (4, 2, 2, 128), (2, 5, 2, 34, 128), (2, 10, 2, 5, 128), (4, 5, 2, 5, 128)]
     return pl.pallas_call(
         exchange_kernel,
         in_specs=[hbm],
         out_specs=[vmem, vmem],
         out_shape=[jax.ShapeDtypeStruct((16, 4, 64, 128), F32), jax.ShapeDtypeStruct((12, 2, 48, 128), F32)],
         scratch_shapes=[pltpu.VMEM(s, F32) for s in shapes]
-        + [pltpu.SemaphoreType.DMA((16 // CHUNK,))]
-        + [pltpu.SemaphoreType.DMA((n,)) for n in (10, 10, 8, 8, 8, 8, len(FAR), len(FAR))],
+        + [pltpu.SemaphoreType.DMA((16 // CHUNK,)), pltpu.SemaphoreType.REGULAR((2,))]
+        + [pltpu.SemaphoreType.DMA((n,)) for n in (14, 14, 8, 8, 8, 8, len(FAR), len(FAR))],
         compiler_params=pltpu.CompilerParams(collective_id=0, has_side_effects=True, vmem_limit_bytes=48 << 20),
     )(pltpu.with_memory_space_constraint(charge, pltpu.HBM))
 
@@ -445,7 +450,7 @@
         for z in range(2):
             for r in range(0, 64, 8):
                 v = [W[2 * i + z, j, pl.ds(r, 8), :] for j in range(4)]
-                for k, w in enumerate(from_groups(v, lane)):
+                for k, w in enumerate(regroup(v, lane)):
                     O[2 * i + z, pl.ds(r, 8), pl.ds(128 * k, 128)] = w
         store(i).start()
         return 0

time: 32.3 us -> 29.7 us (0.920)
  Pallas kernels: 32.1 us -> 29.5 us
    pallas_call x1, Pallas kernels: 28.8 us -> 26.3 us  [exchange(): pl.pallas_call(exchange_kernel, in_specs=[hbm], out_specs=[vmem, vmem], o...]
where the time goes in v2:
time: 29.7 us; the launch traced here: 29.5 us
  Pallas kernels  29.5 us (99%)
    pallas_call x1, Pallas kernels, exchange(): pl.pallas_call(exchange_kernel, in_specs=[hbm], out_specs=[vmem, vmem], o...  26.3 us
    pallas_call x1, Pallas kernels, fine(): pl.pallas_call(fine_kernel, in_specs=[vmem, vmem], out_specs=pl.BlockSpec...  3.23 us

profile of v2, /device:TPU:1, one launch (start us, length us, event | category | flops | bytes accessed | tf_op | source)
XLA Modules:
  0.0 29.5 jit_solution(16107792708197157870)
XLA Ops:
  0.0 26.3 %shard_map.17 = (f32[16,4,64,128]{3,2,1,0:T(8,128)S(1)}, f32[12,2,48,128]{3,2,1,0:T(8,128)S(1)}) custom-call(f32[16,64,512]{2,1,0:T(8,128)} %x_ref.1), custom_call_target="tpu_custom_call" | custom-call | tf_op jit(solution)/shard_map/pallas_call | solution.py:423
  26.3 3.2 %shard_map.18 = f32[16,64,512]{2,1,0:T(8,128)} custom-call(f32[16,4,64,128]{3,2,1,0:T(8,128)S(1)} %get-tuple-element.7.b_ref, f32[12,2,48,128]{3,2,1,0:T(8,128)S(1)} %get-tuple-element.8.q_ref), custom_call_target="tpu_custom_call" | custom-call | tf_op jit(solution)/shard_map/pallas_call | solution.py:465
